TPU v7x, 256 devices: a whole 4x4x8 slice. The times are simulated.
256 devices in a mesh: pair: 2 (over y_lo), narrow: 8 (over x, y_hi), wide: 16 (over z, core).
Axes of the slice: x: 4, y: 4 (y_hi: 2, y_lo: 2; y = y_hi * 2 + y_lo), z: 8, core: 2. Of those that a mesh axis runs over, the one named last changes fastest.
Arguments:
- frame_one: bfloat16 [98304, 128], P(('pair', 'narrow', 'wide')), parts along dimension 0, may hold values from -8 to 8
- frame_two: bfloat16 [98304, 128], P(('pair', 'wide', 'narrow')), parts along dimension 0, may hold values from -8 to 8
Outputs:
- flow_forward: float32 [2, 98304], P(None, ('pair', 'narrow', 'wide')), parts along dimension 1
- flow_backward: float32 [2, 98304], P(None, ('pair', 'wide', 'narrow')), parts along dimension 1
There are 2 independent parts, one for each index of `pair`. A program takes and returns all parts, laid end to end along the dimension named above; each array names one. Nothing has to cross between parts.
All inputs are finite; a program needn't handle non-finite values.
Results may differ from a plain program's by a relative error of at most 0.0003.
Values may be sent and summed in bfloat16 or wider, within the bound.
No kernel may reach another device: no remote copies, remote signals or barrier semaphores. Data moves between devices by JAX's collectives and lax.ppermute only.
A program may use at most 64 MiB of HBM per device.

v0:
```python
import math

import jax
import jax.numpy as jnp
from jax import lax
from jax.sharding import PartitionSpec as P

IMG_W = 384


def combined_all(x, axis, combine):
    everything = jax.tree.map(lambda part: lax.all_gather(part, axis), x)
    initial = jax.tree.map(lambda part: part[0], everything)

    def hop(k, so_far):
        return combine(so_far, jax.tree.map(lambda part: part[k], everything))

    return lax.fori_loop(1, lax.axis_size(axis), hop, initial)


def pixel_coords(first_pixel, count, img_w, img_h):
    pixel_index = first_pixel + jnp.arange(count, dtype=jnp.int32)
    across = (pixel_index % img_w).astype(jnp.float32) * (2.0 / (img_w - 1)) - 1.0
    downward = (pixel_index // img_w).astype(jnp.float32) * (2.0 / (img_h - 1)) - 1.0
    return (across, downward)


def online_tile(queries, query_start, targets, target_x, target_y, backward, score_scale, img_h):
    count = queries.shape[0]
    width = queries.shape[1]
    block_rows = math.gcd(count, 512)
    query_x, query_y = pixel_coords(query_start, count, IMG_W, img_h)
    target_table = jnp.stack([jnp.ones_like(target_x), target_x, target_y], axis=1)
    blocks = (
        queries.reshape(count // block_rows, block_rows, width),
        query_x.reshape(count // block_rows, block_rows),
        query_y.reshape(count // block_rows, block_rows),
    )

    def advance(running, block):
        rows_feat, block_x, block_y = block
        scores = (
            lax.dot_general(
                rows_feat, targets, (((1,), (1,)), ((), ())), preferred_element_type=jnp.float32
            )
            * score_scale
        )
        row_peak = jnp.max(scores, axis=1)
        weights = jnp.exp(scores - row_peak[:, None])
        row_sums = jnp.dot(
            weights,
            target_table,
            precision=lax.Precision.HIGHEST,
            preferred_element_type=jnp.float32,
        )
        forward = (row_peak, row_sums[:, 0], row_sums[:, 1], row_sums[:, 2])
        old_peak, col_total, col_x, col_y = running
        col_peak = jnp.maximum(old_peak, jnp.max(scores, axis=0))
        decay = jnp.exp(old_peak - col_peak)
        col_weights = jnp.exp(scores - col_peak[None, :])
        query_table = jnp.stack([jnp.ones_like(block_x), block_x, block_y])
        col_sums = jnp.dot(
            query_table,
            col_weights,
            precision=lax.Precision.HIGHEST,
            preferred_element_type=jnp.float32,
        )
        running = (
            col_peak,
            col_total * decay + col_sums[0],
            col_x * decay + col_sums[1],
            col_y * decay + col_sums[2],
        )
        return (running, forward)

    backward, forward = lax.scan(advance, backward, blocks)
    forward = tuple((member.reshape(count) for member in forward))
    return (forward, backward)


def combine(first_stats, second_stats):
    peak = jnp.maximum(first_stats[0], second_stats[0])
    left = jnp.exp(first_stats[0] - peak)
    right = jnp.exp(second_stats[0] - peak)
    return (
        peak,
        first_stats[1] * left + second_stats[1] * right,
        first_stats[2] * left + second_stats[2] * right,
        first_stats[3] * left + second_stats[3] * right,
    )


def displacement(sums, own_start, count, img_h):
    across, downward = pixel_coords(own_start, count, IMG_W, img_h)
    return jnp.stack([sums[1] / sums[0] - across, sums[2] / sums[0] - downward])


def on_device(frame_one, frame_two):
    rows_dev, width = frame_one.shape
    n_wide = lax.axis_size("wide")
    n_narrow = lax.axis_size("narrow")
    wide_index = lax.axis_index("wide")
    narrow_index = lax.axis_index("narrow")
    block_one = rows_dev * n_wide
    block_two = rows_dev * n_narrow
    img_h = rows_dev * n_wide * n_narrow // IMG_W
    score_scale = 1.0 / math.sqrt(width)
    start_one = narrow_index * block_one
    start_two = wide_index * block_two
    targets = lax.all_gather(frame_two, "narrow", axis=0, tiled=True)
    target_x, target_y = pixel_coords(start_two, block_two, IMG_W, img_h)
    zero_two = jnp.zeros((block_two,), jnp.float32)
    backward_init = (jnp.full((block_two,), -jnp.inf, jnp.float32), zero_two, zero_two, zero_two)
    queries = lax.all_gather(frame_one, "wide", axis=0, tiled=True)
    forward, backward = online_tile(
        queries, start_one, targets, target_x, target_y, backward_init, score_scale, img_h
    )
    own_one = start_one + wide_index * rows_dev
    own_two = start_two + narrow_index * rows_dev
    forward = combined_all(forward, "wide", combine)
    backward = combined_all(backward, "narrow", combine)
    forward_sums = [
        lax.dynamic_slice_in_dim(member, wide_index * rows_dev, rows_dev) for member in forward[1:]
    ]
    backward_sums = [
        lax.dynamic_slice_in_dim(member, narrow_index * rows_dev, rows_dev)
        for member in backward[1:]
    ]
    flow_forward = displacement(forward_sums, own_one, rows_dev, img_h)
    flow_backward = displacement(backward_sums, own_two, rows_dev, img_h)
    return (flow_forward, flow_backward)


def solution(mesh):
    placed = (P(("pair", "narrow", "wide"), None), P(("pair", "wide", "narrow"), None))
    return jax.shard_map(
        on_device,
        mesh=mesh,
        in_specs=placed,
        out_specs=(P(None, ("pair", "narrow", "wide")), P(None, ("pair", "wide", "narrow"))),
        check_vma=False,
    )
```

profile of v0, /device:TPU:8, one launch (start us, length us, event | category | flops | bytes accessed | tf_op | source)
XLA Modules:
  0.0 416.3 jit_solution(9529401141132257706)
XLA Ops:
  8.2 35.9 %all_gather.43 = bf16[3072,128]{1,0:T(8,128)(2,1)S(1)} all-gather(bf16[384,128]{1,0:T(8,128)(2,1)} %param.9), channel_id=1, replica_groups=mesh['pair'=2,'narrow'=8,'wide'=16] {'narrow'}, dimensions={0}, use_global_device_ids=true | all-gather | bytes 884736 | tf_op jit(solution)/shard_map/all_gather | solution.py:110
  44.2 7.7 %all-gather.10.cloned.1.call-done = bf16[6144,128]{1,0:T(8,128)(2,1)} async-done(((bf16[384,128]{1,0:T(8,128)(2,1)}), bf16[6144,128]{1,0:T(8,128)(2,1)}) %all-gather.10.cloned.1.call-update) | async-done | bytes 1572880 | tf_op jit(solution)/shard_map/all_gather | solution.py:114
  51.9 149.5 %while.69 = (s32[]{:T(128)}, f32[3072]{0:T(1024)S(1)}, f32[3072]{0:T(1024)S(1)}, f32[3072]{0:T(1024)S(1)}, f32[3072]{0:T(1024)S(1)}, /*index=5*/f32[12,512]{1,0:...) while((s32[]{:T(128)}, f32[3072]{0:T(1024)S(1)}, ...), condition=%wide.region_3.4_spmd.clone, body=%wide.region_0.3_spmd.clone.sunk | while | flops 526948864 | bytes 20211952 | solution.py:76
  51.9 2.0 multiply_reduce_fusion.3
  53.9 6.2 %fusion.80 = f32[512,3]{0,1:T(4,128)S(1)} fusion(f32[3072,3]{0,1:T(4,128)S(1)} %get-tuple-element.990, f32[512,3072]{1,0:T(8,128)S(1)} %get-tuple-element.928, f32[512]{0:T(512)S(1)} %get-tuple-element.937), kind=kOutput, calls=%fused_computation.18.clone.1 | convolution fusion | flops 59768832 | bytes 6336512 | tf_op jit(solution)/shard_map/while/body/eval_jaxpr/dot_general | solution.py:50
  60.1 3.8 fusion.77
  64.4 2.0 multiply_reduce_fusion.3
  66.3 6.2 %fusion.80 = f32[512,3]{0,1:T(4,128)S(1)} fusion(f32[3072,3]{0,1:T(4,128)S(1)} %get-tuple-element.990, f32[512,3072]{1,0:T(8,128)S(1)} %get-tuple-element.928, f32[512]{0:T(512)S(1)} %get-tuple-element.937), kind=kOutput, calls=%fused_computation.18.clone.1 | convolution fusion | flops 59768832 | bytes 6336512 | tf_op jit(solution)/shard_map/while/body/eval_jaxpr/dot_general | solution.py:50
  72.6 3.8 fusion.77
  76.8 2.0 multiply_reduce_fusion.3
  78.8 6.2 %fusion.80 = f32[512,3]{0,1:T(4,128)S(1)} fusion(f32[3072,3]{0,1:T(4,128)S(1)} %get-tuple-element.990, f32[512,3072]{1,0:T(8,128)S(1)} %get-tuple-element.928, f32[512]{0:T(512)S(1)} %get-tuple-element.937), kind=kOutput, calls=%fused_computation.18.clone.1 | convolution fusion | flops 59768832 | bytes 6336512 | tf_op jit(solution)/shard_map/while/body/eval_jaxpr/dot_general | solution.py:50
  85.0 3.8 fusion.77
  89.3 2.0 multiply_reduce_fusion.3
  91.3 6.2 %fusion.80 = f32[512,3]{0,1:T(4,128)S(1)} fusion(f32[3072,3]{0,1:T(4,128)S(1)} %get-tuple-element.990, f32[512,3072]{1,0:T(8,128)S(1)} %get-tuple-element.928, f32[512]{0:T(512)S(1)} %get-tuple-element.937), kind=kOutput, calls=%fused_computation.18.clone.1 | convolution fusion | flops 59768832 | bytes 6336512 | tf_op jit(solution)/shard_map/while/body/eval_jaxpr/dot_general | solution.py:50
  97.5 3.8 fusion.77
  101.7 2.0 multiply_reduce_fusion.3
  103.7 6.2 %fusion.80 = f32[512,3]{0,1:T(4,128)S(1)} fusion(f32[3072,3]{0,1:T(4,128)S(1)} %get-tuple-element.990, f32[512,3072]{1,0:T(8,128)S(1)} %get-tuple-element.928, f32[512]{0:T(512)S(1)} %get-tuple-element.937), kind=kOutput, calls=%fused_computation.18.clone.1 | convolution fusion | flops 59768832 | bytes 6336512 | tf_op jit(solution)/shard_map/while/body/eval_jaxpr/dot_general | solution.py:50
  109.9 3.8 fusion.77
  114.2 2.0 multiply_reduce_fusion.3
  116.2 6.2 %fusion.80 = f32[512,3]{0,1:T(4,128)S(1)} fusion(f32[3072,3]{0,1:T(4,128)S(1)} %get-tuple-element.990, f32[512,3072]{1,0:T(8,128)S(1)} %get-tuple-element.928, f32[512]{0:T(512)S(1)} %get-tuple-element.937), kind=kOutput, calls=%fused_computation.18.clone.1 | convolution fusion | flops 59768832 | bytes 6336512 | tf_op jit(solution)/shard_map/while/body/eval_jaxpr/dot_general | solution.py:50
  122.4 3.8 fusion.77
  126.6 2.0 multiply_reduce_fusion.3
  128.6 6.2 %fusion.80 = f32[512,3]{0,1:T(4,128)S(1)} fusion(f32[3072,3]{0,1:T(4,128)S(1)} %get-tuple-element.990, f32[512,3072]{1,0:T(8,128)S(1)} %get-tuple-element.928, f32[512]{0:T(512)S(1)} %get-tuple-element.937), kind=kOutput, calls=%fused_computation.18.clone.1 | convolution fusion | flops 59768832 | bytes 6336512 | tf_op jit(solution)/shard_map/while/body/eval_jaxpr/dot_general | solution.py:50
  134.9 3.8 fusion.77
  139.1 2.0 multiply_reduce_fusion.3
  141.1 6.2 %fusion.80 = f32[512,3]{0,1:T(4,128)S(1)} fusion(f32[3072,3]{0,1:T(4,128)S(1)} %get-tuple-element.990, f32[512,3072]{1,0:T(8,128)S(1)} %get-tuple-element.928, f32[512]{0:T(512)S(1)} %get-tuple-element.937), kind=kOutput, calls=%fused_computation.18.clone.1 | convolution fusion | flops 59768832 | bytes 6336512 | tf_op jit(solution)/shard_map/while/body/eval_jaxpr/dot_general | solution.py:50
  147.3 3.8 fusion.77
  151.6 2.0 multiply_reduce_fusion.3
  153.5 6.2 %fusion.80 = f32[512,3]{0,1:T(4,128)S(1)} fusion(f32[3072,3]{0,1:T(4,128)S(1)} %get-tuple-element.990, f32[512,3072]{1,0:T(8,128)S(1)} %get-tuple-element.928, f32[512]{0:T(512)S(1)} %get-tuple-element.937), kind=kOutput, calls=%fused_computation.18.clone.1 | convolution fusion | flops 59768832 | bytes 6336512 | tf_op jit(solution)/shard_map/while/body/eval_jaxpr/dot_general | solution.py:50
  159.8 3.8 fusion.77
  164.0 2.0 multiply_reduce_fusion.3
  166.0 6.2 %fusion.80 = f32[512,3]{0,1:T(4,128)S(1)} fusion(f32[3072,3]{0,1:T(4,128)S(1)} %get-tuple-element.990, f32[512,3072]{1,0:T(8,128)S(1)} %get-tuple-element.928, f32[512]{0:T(512)S(1)} %get-tuple-element.937), kind=kOutput, calls=%fused_computation.18.clone.1 | convolution fusion | flops 59768832 | bytes 6336512 | tf_op jit(solution)/shard_map/while/body/eval_jaxpr/dot_general | solution.py:50
  172.2 3.8 fusion.77
  176.5 2.0 multiply_reduce_fusion.3
  178.5 6.2 %fusion.80 = f32[512,3]{0,1:T(4,128)S(1)} fusion(f32[3072,3]{0,1:T(4,128)S(1)} %get-tuple-element.990, f32[512,3072]{1,0:T(8,128)S(1)} %get-tuple-element.928, f32[512]{0:T(512)S(1)} %get-tuple-element.937), kind=kOutput, calls=%fused_computation.18.clone.1 | convolution fusion | flops 59768832 | bytes 6336512 | tf_op jit(solution)/shard_map/while/body/eval_jaxpr/dot_general | solution.py:50
  184.7 3.8 fusion.77
  188.9 2.0 multiply_reduce_fusion.3
  190.9 6.2 %fusion.80 = f32[512,3]{0,1:T(4,128)S(1)} fusion(f32[3072,3]{0,1:T(4,128)S(1)} %get-tuple-element.990, f32[512,3072]{1,0:T(8,128)S(1)} %get-tuple-element.928, f32[512]{0:T(512)S(1)} %get-tuple-element.937), kind=kOutput, calls=%fused_computation.18.clone.1 | convolution fusion | flops 59768832 | bytes 6336512 | tf_op jit(solution)/shard_map/while/body/eval_jaxpr/dot_general | solution.py:50
  197.1 3.8 fusion.77
  201.4 34.3 %all-gather = f32[24576]{0:T(1024)S(1)} all-gather(f32[3072]{0:T(1024)S(1)} %get-tuple-element.532), channel_id=2, replica_groups=mesh['pair'=2,'narrow'=8,'wide'=16] {'narrow'}, dimensions={0}, use_global_device_ids=true | all-gather | bytes 110592 | tf_op jit(solution)/shard_map/all_gather | solution.py:12
  235.6 34.2 %all-gather.1 = f32[24576]{0:T(1024)S(1)} all-gather(f32[3072]{0:T(1024)S(1)} %get-tuple-element.533), channel_id=3, replica_groups=mesh['pair'=2,'narrow'=8,'wide'=16] {'narrow'}, dimensions={0}, use_global_device_ids=true | all-gather | bytes 110592 | tf_op jit(solution)/shard_map/all_gather | solution.py:12
  269.9 34.2 %all-gather.2 = f32[24576]{0:T(1024)S(1)} all-gather(f32[3072]{0:T(1024)S(1)} %get-tuple-element.534), channel_id=4, replica_groups=mesh['pair'=2,'narrow'=8,'wide'=16] {'narrow'}, dimensions={0}, use_global_device_ids=true | all-gather | bytes 110592 | tf_op jit(solution)/shard_map/all_gather | solution.py:12
  304.1 34.2 %all-gather.3 = f32[24576]{0:T(1024)S(1)} all-gather(f32[3072]{0:T(1024)S(1)} %get-tuple-element.535), channel_id=5, replica_groups=mesh['pair'=2,'narrow'=8,'wide'=16] {'narrow'}, dimensions={0}, use_global_device_ids=true | all-gather | bytes 110592 | tf_op jit(solution)/shard_map/all_gather | solution.py:12
  338.4 16.6 %all-gather.6 = f32[16,1,6144]{2,1,0:T(1,128)S(1)} all-gather(f32[1,1,6144]{2,1,0:T(1,128)S(1)} %reshape.95), channel_id=1, replica_groups=mesh['pair'=2,'narrow'=8,'wide'=16] {'wide'}, dimensions={0}, use_global_device_ids=true | all-gather | bytes 417792 | tf_op jit(solution)/shard_map/all_gather | solution.py:12
  355.1 15.9 %all-gather.5 = f32[16,1,6144]{2,1,0:T(1,128)S(1)} all-gather(f32[1,1,6144]{2,1,0:T(1,128)S(1)} %reshape.93), channel_id=1, replica_groups=mesh['pair'=2,'narrow'=8,'wide'=16] {'wide'}, dimensions={0}, use_global_device_ids=true | all-gather | bytes 417792 | tf_op jit(solution)/shard_map/all_gather | solution.py:12
  371.2 17.1 %all-gather.4 = f32[16,1,6144]{2,1,0:T(1,128)S(1)} all-gather(f32[1,1,6144]{2,1,0:T(1,128)S(1)} %reshape.91), channel_id=1, replica_groups=mesh['pair'=2,'narrow'=8,'wide'=16] {'wide'}, dimensions={0}, use_global_device_ids=true | all-gather | bytes 417792 | tf_op jit(solution)/shard_map/all_gather | solution.py:12
  388.5 15.5 %all-gather.7 = f32[16,1,6144]{2,1,0:T(1,128)S(1)} all-gather(f32[1,1,6144]{2,1,0:T(1,128)S(1)} %reshape.97), channel_id=1, replica_groups=mesh['pair'=2,'narrow'=8,'wide'=16] {'wide'}, dimensions={0}, use_global_device_ids=true | all-gather | bytes 417792 | tf_op jit(solution)/shard_map/all_gather | solution.py:12
  405.2 2.9 while.67
  (285 shorter events, 10.7 us)
Async XLA Ops:
  7.2 44.7 %all-gather.10.cloned.1.call-start = ((), (), s32[]{:S(2)}) async-start(), calls=%async_computation | async-start | bytes 1671168 | tf_op jit(solution)/shard_map/all_gather | solution.py:114
Sparse Core Ops, SparseCore 0:
  9.8 42.0 all-gather.9
where the time goes:
time: 418 us; the launch traced here: 416 us
  blocking collectives  238 us (57%)
  matrix products  144 us (34%)
  between operations  14.2 us (3%)
  waiting for transfers between devices  8.34 us (2%)
  local copies, waits for them, and re-layouts  6.14 us (1%)
    all_gather x8, blocking collectives, combined_all(): everything = jax.tree.map(lambda part: lax.all_gather(part, axis), x)  202 us
    dot_general x12, matrix products, advance(): jnp.dot(weights, target_table, precision=lax.Precision.HIGHEST, preferred...  74.6 us
    dot_general x12, matrix products, advance(): jnp.dot(query_table, col_weights, precision=lax.Precision.HIGHEST, prefer...  46 us
    all_gather x1, blocking collectives, on_device(): targets = lax.all_gather(frame_two, 'narrow', axis=0, tiled=True)  35.9 us
    dot_general x12, matrix products, advance(): lax.dot_general(rows_feat, targets, (((1,), (1,)), ((), ())), preferred_e...  23.7 us
  transfers between devices with their start and end apart: 1, of which 1 were waited for; matrix products, arithmetic and copies ran while one was open for 0% of the time, Pallas kernels for 0%

commit v1 on v0

v1 whole, which is shorter than its diff:
```python
import functools
import math

import jax
import jax.numpy as jnp
from jax import lax
from jax.experimental import pallas as pl
from jax.experimental.pallas import tpu as pltpu
from jax.sharding import PartitionSpec as P

IMG_W = 384
LANES = 128
THIRDS = IMG_W // LANES
STRIPS = IMG_W // 8
LOWEST = -3.0e38
HIGH = 2.0**100
LOW = 2.0**-80
f32 = jnp.float32
bf16 = jnp.bfloat16
VMEM = pl.BlockSpec(memory_space=pltpu.VMEM)
SMEM = pl.BlockSpec(memory_space=pltpu.SMEM)


def matmul_nt(left, right):
    return lax.dot_general(left, right, (((1,), (1,)), ((), ())), preferred_element_type=f32)


def merged(first, second):
    peak = jnp.maximum(first[0:1], second[0:1])
    sums = first * jnp.exp2(first[0:1] - peak) + second * jnp.exp2(second[0:1] - peak)
    row = lax.broadcasted_iota(jnp.int32, first.shape, 0)
    return jnp.where(row == 0, peak, sums)


def match_kernel(n_rows, n_cols, scale, place, u_ref, v_ref, rows_ref, cols_ref,
                 u2, v2, score, part, flush, peaks, n_col, x_col, y_col, slow_row, slow_col, flags):
    span = n_cols * LANES
    wide = THIRDS * span
    half = n_cols // 2

    def v_order(b):
        return lax.rem(b + place[2] * half, n_cols)

    for b in range(n_cols):
        start = pl.multiple_of(v_order(b) * IMG_W, IMG_W)
        for g in range(THIRDS):
            v2[g, b * LANES:(b + 1) * LANES, :] = v_ref[pl.ds(start + g * LANES, LANES), :]

    def split(a, carry):
        at = pl.ds(pl.multiple_of(a * IMG_W, IMG_W), IMG_W)
        scaled = u_ref[at, :].astype(f32) * scale
        top = scaled.astype(bf16)
        u2[at, :LANES] = top
        u2[at, LANES:] = (scaled - top.astype(f32)).astype(bf16)
        return carry

    lax.fori_loop(0, n_rows, split, 0)

    def clear():
        nothing = jnp.zeros((8, wide), f32)
        n_col[...] = nothing
        x_col[...] = nothing
        y_col[...] = nothing
        slow_col[...] = jnp.where(lax.broadcasted_iota(jnp.int32, (4, wide), 0) == 0, LOWEST, 0.0)

    clear()

    def clear_row():
        slow_row[...] = jnp.where(lax.broadcasted_iota(jnp.int32, (IMG_W, LANES), 1) == 0, LOWEST, 0.0)

    def fast(a, slot):
        left = u2[pl.ds(pl.multiple_of(a * IMG_W, IMG_W), IMG_W), :]
        for g in range(THIRDS):
            top = None
            for t in range(0, span, 512):
                right = v2[g, t:t + 512, :]
                s = matmul_nt(left, jnp.concatenate([right, right], axis=1))
                n = jnp.zeros((8, 512), f32)
                x = jnp.zeros((8, 512), f32)
                for h in range(STRIPS):
                    at = slice(8 * h, 8 * h + 8)
                    e = jnp.exp2(s[at, :])
                    n = n + e
                    x = x + n
                    piece = [e[:, k:k + LANES] for k in range(0, 512, LANES)]
                    if t:
                        run = part[slot, g, at, :LANES] + piece[0]
                        tot = part[slot, g, at, LANES:] + run
                    else:
                        run = piece[0]
                        tot = run
                    for p in piece[1:]:
                        run = run + p
                        tot = tot + run
                    part[slot, g, at, :LANES] = run
                    part[slot, g, at, LANES:] = tot
                flush[slot, g, 0, :, t:t + 512] = n
                flush[slot, g, 1, :, t:t + 512] = x
                m = jnp.maximum(jnp.maximum(n[:, :LANES], n[:, LANES:2 * LANES]),
                                jnp.maximum(n[:, 2 * LANES:3 * LANES], n[:, 3 * LANES:]))
                top = m if top is None else jnp.maximum(top, m)
            peaks[slot, g] = top

    lane = lax.broadcasted_iota(jnp.int32, (1, LANES), 1).astype(f32)
    sub4 = lax.broadcasted_iota(jnp.int32, (4, 3 * LANES), 0)
    third = lax.broadcasted_iota(jnp.int32, (4, 3 * LANES), 1) // LANES
    table = jnp.where(sub4 == third + 1, 1.0, 0.0).astype(bf16)
    table = jnp.concatenate([table, table], axis=1)

    def row_sums(slot):
        n = part[slot, 0, :, :LANES]
        x = n * lane
        y = part[slot, 0, :, LANES:]
        for g in range(1, THIRDS):
            more = part[slot, g, :, :LANES]
            n = n + more
            x = x + more * (lane + g * LANES)
            y = y + part[slot, g, :, LANES:]
        whole = jnp.concatenate([n, x, (place[3] + n_cols).astype(f32) * n - y], axis=1)
        top = whole.astype(bf16)
        rest = (whole - top.astype(f32)).astype(bf16)
        return matmul_nt(table, jnp.concatenate([top, rest], axis=1))

    def slow(a, g):
        left = u2[pl.ds(pl.multiple_of(a * IMG_W, IMG_W), IMG_W), :]
        offset = pl.multiple_of(g * span, span)

        def scores(t, carry):
            at = pl.ds(pl.multiple_of(t * 256, 256), 256)
            right = v2[g, at, :]
            score[:, at] = matmul_nt(left, jnp.concatenate([right, right], axis=1))
            return carry

        lax.fori_loop(0, span // 256, scores, 0)
        index = lax.broadcasted_iota(jnp.int32, (1, span), 1)
        down = (index // LANES + place[3]).astype(f32)
        across = (lax.rem(index, LANES) + g * LANES).astype(f32)
        column = lax.broadcasted_iota(jnp.int32, (64, LANES), 1)

        def by_row(h, peak):
            at = pl.ds(pl.multiple_of(h * 64, 64), 64)
            s = score[at, :]
            m = jnp.max(s, axis=1, keepdims=True)
            w = jnp.exp2(s - m)
            old = slow_row[at, :]
            new = jnp.where(column == 0, m, jnp.where(column == 1, jnp.sum(w, axis=1, keepdims=True), jnp.where(
                column == 2, jnp.sum(w * across, axis=1, keepdims=True), jnp.sum(w * down, axis=1, keepdims=True))))
            both = jnp.maximum(old[:, 0:1], m)
            sums = old * jnp.exp2(old[:, 0:1] - both) + new * jnp.exp2(m - both)
            slow_row[at, :] = jnp.where(column == 0, both, sums)
            for k in range(0, 64, 8):
                peak = jnp.maximum(peak, s[k:k + 8, :])
            return peak

        peak = lax.fori_loop(0, IMG_W // 64, by_row, jnp.full((8, span), LOWEST, f32))
        peak = jnp.max(peak, axis=0, keepdims=True)
        inner = lax.broadcasted_iota(jnp.int32, (8, 1), 0).astype(f32)

        def by_col(h, carry):
            n, x = carry
            for k in range(0, 32, 8):
                w = jnp.exp2(score[pl.ds(pl.multiple_of(h * 32 + k, 8), 8), :] - peak)
                n = n + w
                x = x + w * (inner + (h * 32 + k).astype(f32))
            return n, x

        nothing = jnp.zeros((8, span), f32)
        n, x = lax.fori_loop(0, IMG_W // 32, by_col, (nothing, nothing))
        n = jnp.sum(n, axis=0, keepdims=True)
        x = jnp.sum(x, axis=0, keepdims=True)
        row = lax.broadcasted_iota(jnp.int32, (4, span), 0)
        new = jnp.where(row == 0, peak, jnp.where(row == 1, n, jnp.where(row == 2, x, n * image_row(a))))
        at = pl.ds(offset, span)
        slow_col[:, at] = merged(slow_col[:, at], new)

    def image_row(a):
        return (place[0] + place[1] * a).astype(f32)

    def slow_stats():
        return jnp.transpose(slow_row[...])[0:4]

    def at_zero(stats):
        row = lax.broadcasted_iota(jnp.int32, stats.shape, 0)
        return jnp.where(row == 0, jnp.where(stats[1:2] > 0.0, 0.0, LOWEST), stats)

    def finish(a, slot, real):
        bad = [jnp.logical_not(jnp.max(peaks[slot, g]) < HIGH) for g in range(THIRDS)]
        for g in range(THIRDS):
            at = slice(g * span, (g + 1) * span)
            skip = jnp.logical_or(bad[g], jnp.logical_not(real))
            n = jnp.where(skip, 0.0, flush[slot, g, 0])
            x = jnp.where(skip, 0.0, flush[slot, g, 1])
            n_col[:, at] += n
            x_col[:, at] += x
            y_col[:, at] += n * image_row(a)
        rows_ref[a] = row_sums(slot)
        for g in range(THIRDS):
            flags[g] = bad[g].astype(jnp.int32)
        return jnp.logical_and(real, jnp.logical_or(jnp.logical_or(bad[0], bad[1]), bad[2]))

    def repair(a, slot):
        clear_row()

        def third_of(g, carry):
            @pl.when(flags[g] == 1)
            def _():
                part[slot, g] = jnp.zeros((IMG_W, 2 * LANES), f32)
                slow(a, g)
            return carry

        lax.fori_loop(0, THIRDS, third_of, 0)
        rows_ref[a] = merged(at_zero(row_sums(slot)), slow_stats())

    def body(a, carry):
        slot = lax.rem(a, 2)
        before = jnp.maximum(a - 1, 0)
        other = 1 - slot
        again = finish(before, other, a > 0)
        fast(a, slot)

        @pl.when(again)
        def _():
            repair(before, other)
        return carry

    lax.fori_loop(0, n_rows, body, 0)
    last = n_rows - 1
    again = finish(last, last % 2, last >= 0)

    @pl.when(again)
    def _():
        repair(last, last % 2)

    def columns():
        n = n_col[...]
        inner = lax.broadcasted_iota(jnp.int32, n.shape, 0).astype(f32)
        x = 8.0 * (STRIPS * n - x_col[...]) + n * inner
        row = lax.broadcasted_iota(jnp.int32, (4, wide), 0)
        sums = [jnp.sum(k, axis=0, keepdims=True) for k in (n, x, y_col[...])]
        fast_sums = jnp.where(row == 1, sums[0], jnp.where(row == 2, sums[1], jnp.where(row == 3, sums[2], 0.0)))
        return merged(at_zero(fast_sums), slow_col[...])

    def put(stats):
        for b in range(n_cols):
            to = v_order(b)
            for g in range(THIRDS):
                cols_ref[to, :, g * LANES:(g + 1) * LANES] = stats[:, g * span + b * LANES:g * span + (b + 1) * LANES]

    def least(stats):
        return jnp.min(stats[1:2] * jnp.exp2(stats[0:1]))

    stats = columns()
    put(stats)
    low = least(stats)
    rows_low = rows_ref[0][1:2] * jnp.exp2(rows_ref[0][0:1])
    for a in range(1, n_rows):
        rows_low = jnp.minimum(rows_low, rows_ref[a][1:2] * jnp.exp2(rows_ref[a][0:1]))
    low = jnp.minimum(low, jnp.min(rows_low))

    @pl.when(jnp.logical_not(low >= LOW))
    def _():
        clear()

        def whole_row(a, carry):
            clear_row()

            def one(g, inner):
                slow(a, g)
                return inner

            lax.fori_loop(0, THIRDS, one, 0)
            rows_ref[a] = slow_stats()
            return carry

        lax.fori_loop(0, n_rows, whole_row, 0)
        put(slow_col[...])


def match(place, u, v):
    n_rows, n_cols = u.shape[0] // IMG_W, v.shape[0] // IMG_W
    span = n_cols * LANES
    wide = THIRDS * span
    scale = math.log2(math.e) / math.sqrt(u.shape[1])
    return pl.pallas_call(
        functools.partial(match_kernel, n_rows, n_cols, scale),
        out_shape=(jax.ShapeDtypeStruct((n_rows, 4, IMG_W), f32), jax.ShapeDtypeStruct((n_cols, 4, IMG_W), f32)),
        in_specs=[SMEM, VMEM, VMEM],
        out_specs=(VMEM, VMEM),
        scratch_shapes=[
            pltpu.VMEM((n_rows * IMG_W, 2 * LANES), bf16),
            pltpu.VMEM((THIRDS, span, LANES), bf16),
            pltpu.VMEM((IMG_W, span), f32),
            pltpu.VMEM((2, THIRDS, IMG_W, 2 * LANES), f32),
            pltpu.VMEM((2, THIRDS, 2, 8, span), f32),
            pltpu.VMEM((2, THIRDS, 8, LANES), f32),
            pltpu.VMEM((8, wide), f32),
            pltpu.VMEM((8, wide), f32),
            pltpu.VMEM((8, wide), f32),
            pltpu.VMEM((IMG_W, LANES), f32),
            pltpu.VMEM((4, wide), f32),
            pltpu.SMEM((THIRDS,), jnp.int32),
        ],
        compiler_params=pltpu.CompilerParams(vmem_limit_bytes=56 * 1024 * 1024),
        name="match",
    )(place, u, v)


def merge_kernel(mine, theirs, out):
    for k in range(mine.shape[0]):
        out[k] = merged(mine[k], theirs[k])


def merge(mine, theirs):
    return pl.pallas_call(
        merge_kernel, out_shape=jax.ShapeDtypeStruct(mine.shape, f32), in_specs=[VMEM, VMEM], out_specs=VMEM, name="merge"
    )(mine, theirs)


def flow_kernel(place, one, two, forward, backward):
    across = lax.broadcasted_iota(jnp.int32, (1, IMG_W), 1).astype(f32)
    for k, (stats, out) in enumerate(((one, forward), (two, backward))):
        total = stats[0]
        for other in range(1, stats.shape[0]):
            total = merged(total, stats[other])
        down = place[k].astype(f32)
        out[0:1, :] = (total[2:3] / total[1:2] - across) * (2.0 / (IMG_W - 1))
        out[1:2, :] = (total[3:4] / total[1:2] - down) * (2.0 / (place[2].astype(f32) - 1.0))


def flow(place, one, two):
    out = jax.ShapeDtypeStruct((2, IMG_W), f32)
    return pl.pallas_call(
        flow_kernel, out_shape=(out, out), in_specs=[SMEM, VMEM, VMEM], out_specs=(VMEM, VMEM), name="flow"
    )(place, one, two)


def on_device(frame_one, frame_two):
    n_wide, n_narrow = lax.axis_size("wide"), lax.axis_size("narrow")
    n_z = n_wide // 2
    w, n = lax.axis_index("wide"), lax.axis_index("narrow")
    z, core = w // 2, w % 2
    along_z = [[2 * k + c for k in range(n_z)] for c in range(2)]
    flip = [(k, k ^ 1) for k in range(n_wide)]
    u = lax.all_gather(frame_one, "wide", axis=0, tiled=True, axis_index_groups=along_z)
    v = lax.all_gather(frame_two, "narrow", axis=0, tiled=True)
    v = jnp.concatenate([v, lax.ppermute(v, "wide", flip)], axis=0)
    own_one = n * n_wide + w
    own_two = w * n_narrow + n
    place = jnp.stack([n * n_wide + core, 2, core, 2 * z * n_narrow]).astype(jnp.int32)
    rows, cols = match(place, u, v)
    cols = merge(cols[:n_narrow], lax.ppermute(cols[n_narrow:], "wide", flip))
    rows = lax.all_to_all(rows, "wide", 0, 0, axis_index_groups=along_z)
    cols = lax.all_to_all(cols, "narrow", 0, 0)
    img_h = n_wide * n_narrow
    return flow(jnp.stack([own_one, own_two, img_h]).astype(jnp.int32), rows, cols)


def solution(mesh):
    placed = (P(("pair", "narrow", "wide"), None), P(("pair", "wide", "narrow"), None))
    return jax.shard_map(
        on_device,
        mesh=mesh,
        in_specs=placed,
        out_specs=(P(None, ("pair", "narrow", "wide")), P(None, ("pair", "wide", "narrow"))),
        check_vma=False,
    )
```

time: 418 us -> 134 us (0.32)
  blocking collectives: 238 us -> 67.9 us
  matrix products: 144 us -> 0 us
  Pallas kernels: 0 us -> 37 us
  between operations: 14.2 us -> 0.65 us
  starting transfers between devices: 0.04 us -> 9.66 us
    all_gather x9 -> x2, blocking collectives: 238 us -> 67.9 us  [the longest x1 35.9 us: on_device(): v = lax.all_gather(frame_two, 'narrow', axis=0, tiled=True)]
    dot_general x36 -> x0, matrix products: 144 us -> none  [the longest x12 74.6 us: advance(): jnp.dot(weights, target_table, precision=lax.Precision.HIGHEST, preferred...]
    pallas_call x0 -> x3, Pallas kernels: none -> 37 us  [the longest x1 33.9 us: match(): pl.pallas_call(functools.partial(match_kernel, n_rows, n_cols, scale), ou...]
    all_to_all x0 -> x2, waiting for transfers between devices: none -> 10.5 us  [the longest x1 7.13 us: on_device(): cols = lax.all_to_all(cols, 'narrow', 0, 0)]
    all_to_all x0 -> x2, starting transfers between devices: none -> 9.66 us  [the longest x1 6.31 us: on_device(): cols = lax.all_to_all(cols, 'narrow', 0, 0)]
    all_gather x1 -> x0, waiting for transfers between devices: 7.66 us -> none  [on_device(): queries = lax.all_gather(frame_one, 'wide', axis=0, tiled=True)]
  transfers between devices with their start and end apart: 1 -> 4, of which waited for: 1 -> 3; matrix products, arithmetic and copies ran while one was open for 0% -> 2% of each run, Pallas kernels for 0% -> 1%
where the time goes in v1:
time: 134 us; the launch traced here: 132 us
  blocking collectives  67.9 us (51%)
  Pallas kernels  37 us (28%)
  waiting for transfers between devices  11.7 us (9%)
  starting transfers between devices  9.66 us (7%)
  local copies, waits for them, and re-layouts  2.68 us (2%)
  other arithmetic  2.53 us (2%)
    all_gather x1, blocking collectives, on_device(): v = lax.all_gather(frame_two, 'narrow', axis=0, tiled=True)  35.9 us
    pallas_call x1, Pallas kernels, match(): pl.pallas_call(functools.partial(match_kernel, n_rows, n_cols, scale), ou...  33.9 us
    all_gather x1, blocking collectives, on_device(): lax.all_gather(frame_one, 'wide', axis=0, tiled=True, axis_index_groups=a...  31.9 us
    all_to_all x1, waiting for transfers between devices, on_device(): cols = lax.all_to_all(cols, 'narrow', 0, 0)  7.13 us
    all_to_all x1, starting transfers between devices, on_device(): cols = lax.all_to_all(cols, 'narrow', 0, 0)  6.31 us
    all_to_all x1, starting transfers between devices, on_device(): rows = lax.all_to_all(rows, 'wide', 0, 0, axis_index_groups=along_z)  3.34 us
    all_to_all x1, waiting for transfers between devices, on_device(): rows = lax.all_to_all(rows, 'wide', 0, 0, axis_index_groups=along_z)  3.33 us
  transfers between devices with their start and end apart: 4, of which 3 were waited for; matrix products, arithmetic and copies ran while one was open for 2% of the time, Pallas kernels for 1%

profile of v1, /device:TPU:8, one launch (start us, length us, event | category | flops | bytes accessed | tf_op | source)
XLA Modules:
  0.0 132.1 jit_solution(14457297453079386207)
XLA Ops:
  0.6 35.9 %all_gather.7 = bf16[3072,128]{1,0:T(8,128)(2,1)S(1)} all-gather(bf16[384,128]{1,0:T(8,128)(2,1)} %param.3), channel_id=1, replica_groups=mesh['pair'=2,'narrow'=8,'wide'=16] {'narrow'}, dimensions={0}, use_global_device_ids=true | all-gather | bytes 884736 | tf_op jit(solution)/shard_map/all_gather | solution.py:345
  36.6 0.0 collective-permute-start
  36.6 0.7 pad_add_fusion.1.place
  37.2 31.9 %all_gather.6.u_ref = bf16[3072,128]{1,0:T(8,128)(2,1)} all-gather(bf16[384,128]{1,0:T(8,128)(2,1)} %param.2), channel_id=1, replica_groups={{0,2,4,6,8,10,12,14},{1,3,5,7,9,11,13,15},{16,18,20,22,24,26,28,30},{17..., dimensions={0}, use_global_device_ids=true | all-gather | bytes 884736 | tf_op jit(solution)/shard_map/all_gather | solution.py:344
  69.2 0.0 collective-permute-done
  69.2 1.3 pad_maximum_fusion.v_ref
  70.5 33.9 %match.1 = (f32[8,4,384]{2,1,0:T(4,128)}, f32[16,4,384]{2,1,0:T(4,128)}) custom-call(s32[4]{0:T(128)} %pad_add_fusion.1.place, bf16[3072,128]{1,0:T(8,128)(2,1)} %all_gather.6.u_ref, bf16[6144,128]{1,0:T(8,128)(2,1)} %pad_maximum_fusion.v_ref), custom_call_target="tpu_custom_call" | custom-call | tf_op jit(solution)/shard_map/match/pallas_call | solution.py:284
  104.4 3.3 %all-to-all-start = ((f32[8,4,384]{2,1,0:T(4,128)}), f32[8,4,384]{2,1,0:T(4,128)S(1)}, u32[]{:S(2)}, u32[]{:S(2)}) async-start(f32[8,4,384]{2,1,0:T(4,128)} %get-tuple-element.4), calls=%async_computation | async-start | bytes 98304 | tf_op jit(solution)/shard_map/all_to_all | solution.py:352
  107.7 1.5 %fusion = (f32[8,4,384]{2,1,0:T(4,128)S(1)}, f32[8,4,384]{2,1,0:T(4,128)}) fusion(f32[16,4,384]{2,1,0:T(4,128)} %get-tuple-element.5), kind=kLoop, calls=%fused_computation.3 | loop fusion | bytes 196608 | tf_op jit(solution)/shard_map/slice | solution.py:351
  109.2 0.0 collective-permute-start.1
  109.2 1.2 collective-permute-done.1.theirs
  110.4 0.0 copy-start.2
  110.4 0.6 copy-done.2
  111.0 1.5 %merge.1 = f32[8,4,384]{2,1,0:T(4,128)} custom-call(f32[8,4,384]{2,1,0:T(4,128)} %get-tuple-element.7.mine, f32[8,4,384]{2,1,0:T(4,128)} %copy-done.2), custom_call_target="tpu_custom_call" | custom-call | tf_op jit(solution)/shard_map/merge/pallas_call | solution.py:314
  112.5 3.3 %all-to-all-done.one = f32[8,4,384]{2,1,0:T(4,128)S(1)} async-done(((f32[8,4,384]{2,1,0:T(4,128)}), f32[8,4,384]{2,1,0:T(4,128)S(1)}, u32[]{:S(2)}, u32[]{:S(2)}) %all-to-all-start) | async-done | bytes 49184 | tf_op jit(solution)/shard_map/all_to_all | solution.py:352
  115.8 0.0 copy-start
  115.8 6.3 %all-to-all-start.1 = ((f32[8,4,384]{2,1,0:T(4,128)}), f32[8,4,384]{2,1,0:T(4,128)S(1)}, u32[]{:S(2)}, u32[]{:S(2)}) async-start(f32[8,4,384]{2,1,0:T(4,128)} %merge.1), calls=%async_computation.1 | async-start | bytes 98304 | tf_op jit(solution)/shard_map/all_to_all | solution.py:353
  122.2 0.6 pad_add_fusion.place
  122.8 7.1 %all-to-all-done.1.two = f32[8,4,384]{2,1,0:T(4,128)S(1)} async-done(((f32[8,4,384]{2,1,0:T(4,128)}), f32[8,4,384]{2,1,0:T(4,128)S(1)}, u32[]{:S(2)}, u32[]{:S(2)}) %all-to-all-start.1) | async-done | bytes 49184 | tf_op jit(solution)/shard_map/all_to_all | solution.py:353
  129.9 0.0 copy-done
  129.9 0.0 copy-start.1
  129.9 0.6 copy-done.1
  130.5 1.6 %flow.1 = (f32[2,384]{1,0:T(2,128)}, f32[2,384]{1,0:T(2,128)}) custom-call(s32[3]{0:T(128)} %pad_add_fusion.place, f32[8,4,384]{2,1,0:T(4,128)} %copy-done, f32[8,4,384]{2,1,0:T(4,128)} %copy-done.1), custom_call_target="tpu_custom_call" | custom-call | tf_op jit(solution)/shard_map/flow/pallas_call | solution.py:332
Async XLA Ops:
  36.6 32.6 %collective-permute-start = (bf16[3072,128]{1,0:T(8,128)(2,1)S(1)}, bf16[3072,128]{1,0:T(8,128)(2,1)S(1)}, u32[]{:S(2)}, u32[]{:S(2)}) collective-permute-start(bf16[3072,128]{1,0:T(8,128)(2,1)S(1)} %all_gather.7), channel_id=1, source_target_pairs={{0,1},{1,0},{2,3},{3,2},{4,5},{5,4},{6,7},{7,6},{8,9},{9,8},{10,11... | collective-permute-start | bytes 2359304 | tf_op jit(solution)/shard_map/ppermute | solution.py:346
  104.4 11.5 %all-to-all-start = ((f32[8,4,384]{2,1,0:T(4,128)}), f32[8,4,384]{2,1,0:T(4,128)S(1)}, u32[]{:S(2)}, u32[]{:S(2)}) async-start(f32[8,4,384]{2,1,0:T(4,128)} %get-tuple-element.4), calls=%async_computation | async-start | bytes 98304 | tf_op jit(solution)/shard_map/all_to_all | solution.py:352
  109.2 1.2 collective-permute-start.1
  110.4 0.6 copy-start.2
  115.8 14.1 %copy-start = (f32[8,4,384]{2,1,0:T(4,128)}, f32[8,4,384]{2,1,0:T(4,128)S(1)}, u32[]{:S(2)}) copy-start(f32[8,4,384]{2,1,0:T(4,128)S(1)} %all-to-all-done.one) | copy-start | bytes 147460
  115.8 14.1 %all-to-all-start.1 = ((f32[8,4,384]{2,1,0:T(4,128)}), f32[8,4,384]{2,1,0:T(4,128)S(1)}, u32[]{:S(2)}, u32[]{:S(2)}) async-start(f32[8,4,384]{2,1,0:T(4,128)} %merge.1), calls=%async_computation.1 | async-start | bytes 98304 | tf_op jit(solution)/shard_map/all_to_all | solution.py:353
  129.9 0.6 copy-start.1
